TPU v7x, 256 devices: a whole 4x4x8 slice. The times are simulated.
256 devices in a mesh: row: 32 (over y, x, core), col: 8 (over z).
Axes of the slice: x: 4, y: 4, z: 8, core: 2. Of those that a mesh axis runs over, the one named last changes fastest.
Arguments:
- features: bfloat16 [524288, 256], P(('row', 'col')), may hold values from -6 to 6
- w_self: bfloat16 [256, 256], replicated, may hold values from -0.375 to 0.375
- w_neigh: bfloat16 [256, 256], replicated, may hold values from -1.5 to 1.5
- bias: float32 [256], replicated, may hold values from -3 to 3
- hub_ids: int32 [6], replicated, may hold values from 0 to 31
- hub_adj: bfloat16 [256, 6, 2048, 256], P(('row', 'col')), may hold values from 0 to 2, as said below
- send_tile: int32 [256, 8, 2], P(('row', 'col')), may hold values from 0 to 15
- recv_count: int32 [256, 8], P(('row', 'col')), may hold values from 0 to 2, as said below
- recv_dst: int32 [256, 8, 2], P(('row', 'col')), may hold values from 0 to 15
- recv_adj: bfloat16 [256, 8, 2, 128, 128], P(('row', 'col')), may hold values from 0 to 2, as said below
- cotangent: bfloat16 [524288, 256], P(('row', 'col')), may hold values from -6 to 6
Outputs:
- output: bfloat16 [524288, 256], P(('row', 'col'))
- feature_grad: bfloat16 [524288, 256], P(('row', 'col'))
Inputs may be any that keep to these rules, and one draw needn't show every extreme that they name: `recv_count`: every device uses all 2 slots from at least one device of its row group. `hub_adj`: nonnegative edge weights. `recv_adj`: nonnegative edge weights.
All inputs are finite; a program needn't handle non-finite values.
Results may differ from a plain program's by a relative error of at most 0.0055.
Values may be sent and summed in bfloat16 or wider, within the bound.
A program may use at most 64 MiB of HBM per device.

v0:
```python
import jax
import jax.numpy as jnp
from jax import lax
from jax.sharding import PartitionSpec as P


def shards(
    features,
    w_self,
    w_neigh,
    bias,
    hub_ids,
    hub_adj,
    send_tile,
    recv_count,
    recv_dst,
    recv_adj,
    cotangent,
):
    f32 = jnp.float32
    bf16 = jnp.bfloat16
    nodes, width = features.shape
    sections = hub_ids.shape[0]
    hub_rows = hub_adj.shape[3]
    peers, slots, tile = (recv_adj.shape[1], recv_adj.shape[2], recv_adj.shape[3])
    total = peers * slots
    count_tiles = nodes // tile
    adjacency = hub_adj[0]
    rows_n = lax.axis_size("row")
    part = hub_rows // rows_n
    pieces = lax.all_to_all(
        features[:hub_rows].reshape(rows_n, part, width),
        "row",
        split_axis=0,
        concat_axis=0,
        tiled=True,
    )
    picked = jnp.stack(
        [lax.dynamic_index_in_dim(pieces, hub_ids[s], 0, keepdims=False) for s in range(sections)]
    )
    gathered = lax.all_gather(picked, "row", axis=0, tiled=False)
    blocks = jnp.transpose(gathered, (1, 0, 2, 3)).reshape(sections, hub_rows, width)
    hub_sum = jnp.zeros((nodes, width), f32)
    for section in range(sections):
        hub_sum = hub_sum + jnp.dot(adjacency[section], blocks[section], preferred_element_type=f32)
    offered = send_tile[0].reshape(total)
    outgoing = jnp.stack(
        [lax.dynamic_slice_in_dim(features, offered[i] * tile, tile, 0) for i in range(total)]
    ).reshape(peers, slots, tile, width)
    incoming = lax.all_to_all(outgoing, "col", split_axis=0, concat_axis=0, tiled=True)
    live = (
        (jnp.arange(slots, dtype=jnp.int32)[None, :] < recv_count[0][:, None])
        .astype(f32)
        .reshape(total)
    )
    landing = recv_dst[0].reshape(total)
    select = (landing[:, None] == jnp.arange(count_tiles, dtype=jnp.int32)[None, :]).astype(
        f32
    ) * live[:, None]
    weights = recv_adj[0].reshape(total, tile, tile)
    contrib = jnp.einsum(
        "sij,sjd->sid", weights, incoming.reshape(total, tile, width), preferred_element_type=f32
    )
    tile_sum = jnp.einsum("sn,sid->nid", select, contrib, precision=lax.Precision.HIGHEST).reshape(
        nodes, width
    )
    row_weight = jnp.sum(weights.astype(f32), axis=2)
    tile_deg = jnp.einsum("sn,si->ni", select, row_weight, precision=lax.Precision.HIGHEST).reshape(
        nodes
    )
    degree = 1.0 + jnp.sum(adjacency.astype(f32), axis=(0, 2)) + tile_deg
    agg = ((tile_sum + hub_sum) / degree[:, None]).astype(bf16)
    pre = (
        jnp.dot(features, w_self, preferred_element_type=f32)
        + jnp.dot(agg, w_neigh, preferred_element_type=f32)
        + bias
    )
    sig = jax.nn.sigmoid(pre)
    output = (pre * sig).astype(bf16)
    grad = (cotangent.astype(f32) * sig * (1.0 + pre * (1.0 - sig))).astype(bf16)
    contract = (((1,), (1,)), ((), ()))
    self_grad = lax.dot_general(grad, w_self, contract, preferred_element_type=f32)
    agg_grad = (
        lax.dot_general(grad, w_neigh, contract, preferred_element_type=f32) / degree[:, None]
    ).astype(bf16)
    partials = jnp.stack(
        [
            lax.dot_general(
                adjacency[section], agg_grad, (((0,), (0,)), ((), ())), preferred_element_type=f32
            ).astype(bf16)
            for section in range(sections)
        ]
    ).reshape(sections, rows_n, part, width)
    landed = lax.all_to_all(partials, "row", split_axis=1, concat_axis=1, tiled=True)
    summed = jnp.sum(landed.astype(f32), axis=1)
    owners = (hub_ids[None, :] == jnp.arange(rows_n, dtype=jnp.int32)[:, None]).astype(f32)
    to_owner = jnp.sum(owners[:, :, None, None] * summed[None], axis=1).astype(bf16)
    hub_back = (
        lax.all_to_all(to_owner, "row", split_axis=0, concat_axis=0, tiled=True)
        .astype(f32)
        .reshape(hub_rows, width)
    )
    dest_rows = jnp.stack(
        [lax.dynamic_slice_in_dim(agg_grad, landing[i] * tile, tile, 0) for i in range(total)]
    )
    slot_grad = (
        jnp.einsum("sij,sid->sjd", weights, dest_rows, preferred_element_type=f32)
        * live[:, None, None]
    ).astype(bf16)
    returned = lax.all_to_all(
        slot_grad.reshape(peers, slots, tile, width), "col", split_axis=0, concat_axis=0, tiled=True
    )
    owned = (offered[:, None] == jnp.arange(count_tiles, dtype=jnp.int32)[None, :]).astype(f32)
    tile_back = jnp.einsum(
        "sn,sid->nid",
        owned,
        returned.reshape(total, tile, width).astype(f32),
        precision=lax.Precision.HIGHEST,
    ).reshape(nodes, width)
    hub_padded = jnp.concatenate([hub_back, jnp.zeros((nodes - hub_rows, width), f32)], axis=0)
    feature_grad = (self_grad + tile_back + hub_padded).astype(bf16)
    return (output, feature_grad)


def solution(mesh):
    placed = (
        P(("row", "col"), None),
        P(),
        P(),
        P(),
        P(),
        P(("row", "col"), None, None, None),
        P(("row", "col"), None, None),
        P(("row", "col"), None),
        P(("row", "col"), None, None),
        P(("row", "col"), None, None, None, None),
        P(("row", "col"), None),
    )
    return jax.shard_map(
        shards,
        mesh=mesh,
        in_specs=placed,
        out_specs=(P(("row", "col"), None), P(("row", "col"), None)),
        check_vma=False,
    )
```

profile of v0, /device:TPU:1, one launch (start us, length us, event | category | flops | bytes accessed | tf_op | source)
XLA Modules:
  0.0 204.4 jit_solution(7526366855033646529)
XLA Ops:
  0.7 1.7 slice_bitcast_fusion.13
  2.3 8.6 %all-to-all-start.1 = ((bf16[32,8,256]{2,1,0:T(8,128)(2,1)}), bf16[32,8,256]{2,1,0:T(8,128)(2,1)S(1)}, u32[]{:S(2)}, u32[]{:S(2)}) async-start(bf16[32,8,256]{2,1,0:T(8,128)(2,1)} %slice_bitcast_fusion.13), calls=%async_computation.1 | async-start | bytes 262144 | tf_op jit(solution)/shard_map/all_to_all | solution.py:31
  10.9 0.8 copy.132
  22.6 1.6 fusion.66
  43.1 0.9 constant_dynamic-update-slice_fusion.15
  44.0 0.8 constant_dynamic-update-slice_fusion.14
  44.9 0.8 constant_dynamic-update-slice_fusion.13
  45.7 0.8 constant_dynamic-update-slice_fusion.12
  46.6 0.8 constant_dynamic-update-slice_fusion.11
  47.4 0.8 constant_dynamic-update-slice_fusion.10
  48.3 0.8 constant_dynamic-update-slice_fusion.9
  49.1 0.8 constant_dynamic-update-slice_fusion.8
  49.9 0.8 constant_dynamic-update-slice_fusion.7
  50.9 1.3 copy.133
  52.7 3.7 %convert_reduce_fusion = f32[2048]{0:T(1024)S(1)} fusion(bf16[1,6,2048,256]{3,2,1,0:T(8,128)(2,1)} %param.16), kind=kLoop, calls=%fused_computation | loop fusion | flops 6289408 | bytes 6299648 | tf_op jit(solution)/shard_map/reduce_sum | solution.py:71
  56.4 1.8 fusion.70
  62.2 8.3 %all-to-all-start = ((bf16[8,2,128,256]{2,3,1,0:T(8,128)(2,1)}), bf16[8,2,128,256]{2,3,1,0:T(8,128)(2,1)}, u32[]{:S(2)}, u32[]{:S(2)}) async-start(bf16[8,2,128,256]{2,3,1,0:T(8,128)(2,1)} %copy.133), calls=%async_computation | async-start | bytes 2097152 | tf_op jit(solution)/shard_map/all_to_all | solution.py:50
  70.6 25.5 %all-gather = bf16[192,8,256]{2,1,0:T(8,128)(2,1)S(1)} all-gather(bf16[6,8,256]{2,1,0:T(8,128)(2,1)S(1)} %constant_dynamic-update-slice_fusion.16), channel_id=2, replica_groups=mesh['row'=32,'col'=8] {'row'}, dimensions={0}, use_global_device_ids=true | all-gather | bytes 811008 | tf_op jit(solution)/shard_map/all_gather | solution.py:41
  96.1 1.9 fusion.33
  98.0 1.7 convolution_add_fusion.6
  100.8 1.8 convolution_add_fusion.3
  102.6 3.0 %convolution_bitcast_fusion = f32[16,128,256]{1,2,0:T(8,128)} fusion(bf16[16,128,256]{1,2,0:T(8,128)(2,1)} %bitcast.35, bf16[16,128,128]{2,1,0:T(8,128)(2,1)S(1)} %bitcast.269), kind=kOutput, calls=%fused_computation.21 | convolution fusion | flops 134217728 | bytes 3670016 | tf_op jit(solution)/shard_map/sij,sjd->sid/dot_general | solution.py:61
  105.6 2.2 %copy.134 = f32[16,128,256]{2,0,1:T(8,128)S(1)} copy(f32[16,128,256]{1,2,0:T(8,128)} %convolution_bitcast_fusion) | data formatting | bytes 4194304 | tf_op jit(solution)/shard_map/sij,sjd->sid/dot_general | solution.py:61
  107.9 2.5 %fusion.51 = f32[16,128,256]{2,0,1:T(8,128)S(1)} fusion(f32[16,128,256]{2,0,1:T(8,128)S(1)} %copy.134, f32[16]{0:T(128)} %copy-done.10, s32[16]{0:T(128)S(1)} %eq.45), kind=kOutput, calls=%fused_computation.126 | convolution fusion | flops 100663808 | bytes 4194432 | tf_op jit(solution)/shard_map/sn,sid->nid/dot_general | solution.py:64
  110.4 1.2 copy.135
  111.6 1.9 copy.136
  113.5 6.0 %multiply_convert_fusion.1 = (bf16[2048,256]{1,0:T(8,128)(2,1)S(1)}, bf16[2048,256]{1,0:T(8,128)(2,1)}) fusion(bf16[2048,256]{1,0:T(8,128)(2,1)} %param.21, f32[256]{0:T(256)S(1)} %copy-done.13, f32[2048,256]{1,0:T(8,128)} %fusion.70, bf16[256,256]{1,0:T(8,128)(2,1)S(1)} %copy-done, f32[2048,256]{0,1:T(8,128)} %copy.136, ...), kind=kOutput, calls=%fused_computation.18 | convolution fusion | flops 546308096 | bytes 10757120 | tf_op jit(solution)/shard_map/dot_general | solution.py:75
  120.4 2.8 %fusion.9 = bf16[6,32,8,256]{3,2,0,1:T(8,128)(2,1)} fusion(bf16[2048,256]{0,1:T(8,128)(2,1)S(1)} %fusion.5, bf16[1,6,2048,256]{3,2,1,0:T(8,128)(2,1)} %param.16), kind=kOutput, calls=%fused_computation.31 | convolution fusion | flops 268500992 | bytes 2228224 | tf_op jit(solution)/shard_map/dot_general | solution.py:88
  123.2 2.4 %fusion.11 = bf16[6,32,8,256]{3,2,0,1:T(8,128)(2,1)} fusion(bf16[6,32,8,256]{3,2,0,1:T(8,128)(2,1)} %fusion.9, bf16[2048,256]{0,1:T(8,128)(2,1)S(1)} %fusion.5, bf16[1,6,2048,256]{3,2,1,0:T(8,128)(2,1)} %param.16), kind=kOutput, calls=%fused_computation.33 | convolution fusion | flops 268500992 | bytes 2228224 | tf_op jit(solution)/shard_map/dot_general | solution.py:88
  125.6 2.4 %fusion.13 = bf16[6,32,8,256]{3,2,0,1:T(8,128)(2,1)} fusion(bf16[6,32,8,256]{3,2,0,1:T(8,128)(2,1)} %fusion.11, bf16[2048,256]{0,1:T(8,128)(2,1)S(1)} %fusion.5, bf16[1,6,2048,256]{3,2,1,0:T(8,128)(2,1)} %param.16), kind=kOutput, calls=%fused_computation.35 | convolution fusion | flops 268500992 | bytes 2228224 | tf_op jit(solution)/shard_map/dot_general | solution.py:88
  128.1 2.4 %fusion.15 = bf16[6,32,8,256]{3,2,0,1:T(8,128)(2,1)} fusion(bf16[6,32,8,256]{3,2,0,1:T(8,128)(2,1)} %fusion.13, bf16[2048,256]{0,1:T(8,128)(2,1)S(1)} %fusion.5, bf16[1,6,2048,256]{3,2,1,0:T(8,128)(2,1)} %param.16), kind=kOutput, calls=%fused_computation.37 | convolution fusion | flops 268500992 | bytes 2228224 | tf_op jit(solution)/shard_map/dot_general | solution.py:88
  130.5 2.4 %fusion.17 = bf16[6,32,8,256]{3,2,0,1:T(8,128)(2,1)} fusion(bf16[6,32,8,256]{3,2,0,1:T(8,128)(2,1)} %fusion.15, bf16[2048,256]{0,1:T(8,128)(2,1)S(1)} %fusion.5, bf16[1,6,2048,256]{3,2,1,0:T(8,128)(2,1)} %param.16), kind=kOutput, calls=%fused_computation.39 | convolution fusion | flops 268500992 | bytes 2228224 | tf_op jit(solution)/shard_map/dot_general | solution.py:88
  132.9 2.4 %fusion.19 = bf16[6,32,8,256]{3,2,0,1:T(8,128)(2,1)} fusion(bf16[6,32,8,256]{3,2,0,1:T(8,128)(2,1)} %fusion.17, bf16[2048,256]{0,1:T(8,128)(2,1)S(1)} %fusion.5, bf16[1,6,2048,256]{3,2,1,0:T(8,128)(2,1)} %param.16), kind=kOutput, calls=%fused_computation.41 | convolution fusion | flops 268500992 | bytes 2228224 | tf_op jit(solution)/shard_map/dot_general | solution.py:88
  135.3 5.2 %all-to-all-start.3 = ((bf16[6,32,8,256]{3,2,0,1:T(8,128)(2,1)}), bf16[6,32,8,256]{3,2,0,1:T(8,128)(2,1)S(1)}, u32[]{:S(2)}, u32[]{:S(2)}) async-start(bf16[6,32,8,256]{3,2,0,1:T(8,128)(2,1)} %fusion.19), calls=%async_computation.3 | async-start | bytes 1572864 | tf_op jit(solution)/shard_map/all_to_all | solution.py:94
  140.6 0.9 constant_dynamic-update-slice_fusion.37
  141.4 0.9 constant_dynamic-update-slice_fusion.36
  142.3 0.9 constant_dynamic-update-slice_fusion.35
  143.1 0.9 constant_dynamic-update-slice_fusion.34
  144.5 1.4 multiply_convert_fusion
  145.9 8.9 %all-to-all-done.3 = bf16[6,32,8,256]{3,2,0,1:T(8,128)(2,1)S(1)} async-done(((bf16[6,32,8,256]{3,2,0,1:T(8,128)(2,1)}), bf16[6,32,8,256]{3,2,0,1:T(8,128)(2,1)S(1)}, u32[]{:S(2)}, u32[]{:S(2)}) %all-to-all-start.3) | async-done | bytes 786464 | tf_op jit(solution)/shard_map/all_to_all | solution.py:94
  154.8 6.9 %all-to-all-start.2 = ((bf16[8,2,128,256]{2,3,1,0:T(8,128)(2,1)}), bf16[8,2,128,256]{2,3,1,0:T(8,128)(2,1)S(1)}, u32[]{:S(2)}, u32[]{:S(2)}) async-start(bf16[8,2,128,256]{2,3,1,0:T(8,128)(2,1)} %bitcast.98), calls=%async_computation.2 | async-start | bytes 2097152 | tf_op jit(solution)/shard_map/all_to_all | solution.py:110
  161.9 0.9 multiply_reduce_fusion
  162.8 28.2 %all-to-all-done.2 = bf16[8,2,128,256]{2,3,1,0:T(8,128)(2,1)S(1)} async-done(((bf16[8,2,128,256]{2,3,1,0:T(8,128)(2,1)}), bf16[8,2,128,256]{2,3,1,0:T(8,128)(2,1)S(1)}, u32[]{:S(2)}, u32[]{:S(2)}) %all-to-all-start.2) | async-done | bytes 1048608 | tf_op jit(solution)/shard_map/all_to_all | solution.py:110
  190.9 4.3 %all-to-all-start.4 = ((bf16[32,8,256]{2,1,0:T(8,128)(2,1)}), bf16[32,8,256]{2,1,0:T(8,128)(2,1)S(1)}, u32[]{:S(2)}, u32[]{:S(2)}) async-start(bf16[32,8,256]{2,1,0:T(8,128)(2,1)} %multiply_reduce_fusion), calls=%async_computation.4 | async-start | bytes 262144 | tf_op jit(solution)/shard_map/all_to_all | solution.py:99
  195.3 0.9 copy.195
  196.6 1.2 copy.171
  197.9 5.0 %all-to-all-done.4 = bf16[32,8,256]{2,1,0:T(8,128)(2,1)S(1)} async-done(((bf16[32,8,256]{2,1,0:T(8,128)(2,1)}), bf16[32,8,256]{2,1,0:T(8,128)(2,1)S(1)}, u32[]{:S(2)}, u32[]{:S(2)}) %all-to-all-start.4) | async-done | bytes 131104 | tf_op jit(solution)/shard_map/all_to_all | solution.py:99
  202.9 1.4 fusion.4
  (75 shorter events, 6.1 us)
Async XLA Ops:
  0.6 112.9 %copy-start = (bf16[256,256]{1,0:T(8,128)(2,1)S(1)}, bf16[256,256]{1,0:T(8,128)(2,1)}, u32[]{:S(2)}) copy-start(bf16[256,256]{1,0:T(8,128)(2,1)} %param.13) | copy-start | bytes 393220
  0.6 50.1 %copy-start.1 = (bf16[2048,256]{1,0:T(8,128)(2,1)S(1)}, bf16[2048,256]{1,0:T(8,128)(2,1)}, u32[]{:S(2)}) copy-start(bf16[2048,256]{1,0:T(8,128)(2,1)} %param.11) | copy-start | bytes 3145732
  2.3 59.8 %all-to-all-start.1 = ((bf16[32,8,256]{2,1,0:T(8,128)(2,1)}), bf16[32,8,256]{2,1,0:T(8,128)(2,1)S(1)}, u32[]{:S(2)}, u32[]{:S(2)}) async-start(bf16[32,8,256]{2,1,0:T(8,128)(2,1)} %slice_bitcast_fusion.13), calls=%async_computation.1 | async-start | bytes 262144 | tf_op jit(solution)/shard_map/all_to_all | solution.py:31
  43.1 9.2 %copy-start.12 = (s32[1,8]{1,0:T(1,128)S(1)}, s32[1,8]{1,0:T(1,128)}, u32[]{:S(2)}) copy-start(s32[1,8]{1,0:T(1,128)} %param.18) | copy-start | bytes 100
  43.1 9.3 %copy-start.2 = (bf16[1,8,2,128,128]{4,3,2,1,0:T(8,128)(2,1)S(1)}, bf16[1,8,2,128,128]{4,3,2,1,0:T(8,128)(2,1)}, u32[]{:S(2)}) copy-start(bf16[1,8,2,128,128]{4,3,2,1,0:T(8,128)(2,1)} %param.20) | copy-start | bytes 1572868
  52.4 9.6 %copy-start.10 = (f32[16]{0:T(128)}, f32[16]{0:T(128)S(1)}, u32[]{:S(2)}) copy-start(f32[16]{0:T(128)S(1)} %reshape.208) | copy-start | bytes 196
  52.6 3.7 %copy-start.7 = (bf16[256,256]{1,0:T(8,128)(2,1)S(1)}, bf16[256,256]{1,0:T(8,128)(2,1)}, u32[]{:S(2)}) copy-start(bf16[256,256]{1,0:T(8,128)(2,1)} %param.12) | copy-start | bytes 393220
  62.2 37.6 %slice-start = ((s8[6291456]{0:T(1024)(128)(4,1)}), s8[2097152]{0:T(1024)(128)(4,1)S(1)}, s32[]{:S(2)}) async-start(s8[6291456]{0:T(1024)(128)(4,1)} %bitcast.265), calls=%async_computation.5 | async-start | bytes 4194304
  62.2 40.4 %all-to-all-start = ((bf16[8,2,128,256]{2,3,1,0:T(8,128)(2,1)}), bf16[8,2,128,256]{2,3,1,0:T(8,128)(2,1)}, u32[]{:S(2)}, u32[]{:S(2)}) async-start(bf16[8,2,128,256]{2,3,1,0:T(8,128)(2,1)} %copy.133), calls=%async_computation | async-start | bytes 2097152 | tf_op jit(solution)/shard_map/all_to_all | solution.py:50
  96.1 3.6 %slice-start.1 = ((s8[6291456]{0:T(1024)(128)(4,1)}), s8[4194304]{0:T(1024)(128)(4,1)S(1)}, s32[]{:S(2)}) async-start(s8[6291456]{0:T(1024)(128)(4,1)} %bitcast.265), calls=%async_computation.6 | async-start | bytes 8388608
  111.6 1.9 copy-start.13
  119.5 1.0 copy-start.3
  120.4 12.4 %copy-start.5 = (bf16[2048,256]{0,1:T(8,128)(2,1)}, bf16[2048,256]{0,1:T(8,128)(2,1)S(1)}, u32[]{:S(2)}) copy-start(bf16[2048,256]{0,1:T(8,128)(2,1)S(1)} %fusion.5) | copy-start | bytes 3145732
  135.3 8.7 %copy-start.6 = (bf16[2048,256]{0,1:T(8,128)(2,1)S(1)}, bf16[2048,256]{0,1:T(8,128)(2,1)}, u32[]{:S(2)}) copy-start(bf16[2048,256]{0,1:T(8,128)(2,1)} %copy-done.5) | copy-start | bytes 3145732
  135.3 9.2 %copy-start.11 = (f32[16]{0:T(128)S(1)}, f32[16]{0:T(128)}, u32[]{:S(2)}) copy-start(f32[16]{0:T(128)} %copy-done.10) | copy-start | bytes 196
  135.3 19.5 %all-to-all-start.3 = ((bf16[6,32,8,256]{3,2,0,1:T(8,128)(2,1)}), bf16[6,32,8,256]{3,2,0,1:T(8,128)(2,1)S(1)}, u32[]{:S(2)}, u32[]{:S(2)}) async-start(bf16[6,32,8,256]{3,2,0,1:T(8,128)(2,1)} %fusion.19), calls=%async_computation.3 | async-start | bytes 1572864 | tf_op jit(solution)/shard_map/all_to_all | solution.py:94
  144.5 17.2 %copy-start.9 = (s32[6]{0:T(128)S(1)}, s32[6]{0:T(128)}, u32[]{:S(2)}) copy-start(s32[6]{0:T(128)} %param.15) | copy-start | bytes 76
  154.8 36.2 %all-to-all-start.2 = ((bf16[8,2,128,256]{2,3,1,0:T(8,128)(2,1)}), bf16[8,2,128,256]{2,3,1,0:T(8,128)(2,1)S(1)}, u32[]{:S(2)}, u32[]{:S(2)}) async-start(bf16[8,2,128,256]{2,3,1,0:T(8,128)(2,1)} %bitcast.98), calls=%async_computation.2 | async-start | bytes 2097152 | tf_op jit(solution)/shard_map/all_to_all | solution.py:110
  190.9 12.0 %all-to-all-start.4 = ((bf16[32,8,256]{2,1,0:T(8,128)(2,1)}), bf16[32,8,256]{2,1,0:T(8,128)(2,1)S(1)}, u32[]{:S(2)}, u32[]{:S(2)}) async-start(bf16[32,8,256]{2,1,0:T(8,128)(2,1)} %multiply_reduce_fusion), calls=%async_computation.4 | async-start | bytes 262144 | tf_op jit(solution)/shard_map/all_to_all | solution.py:99
  196.6 6.3 %copy-start.4 = (bf16[2048,256]{1,0:T(8,128)(2,1)S(1)}, bf16[2048,256]{1,0:T(8,128)(2,1)}, u32[]{:S(2)}) copy-start(bf16[2048,256]{1,0:T(8,128)(2,1)} %copy-done.3) | copy-start | bytes 3145732
  196.6 6.3 %copy-start.8 = (bf16[256,256]{1,0:T(8,128)(2,1)S(1)}, bf16[256,256]{1,0:T(8,128)(2,1)}, u32[]{:S(2)}) copy-start(bf16[256,256]{1,0:T(8,128)(2,1)} %param.12) | copy-start | bytes 393220
where the time goes:
time: 206 us; the launch traced here: 204 us
  waiting for transfers between devices  42.1 us (20%)
  matrix products  38.4 us (19%)
  starting transfers between devices  33.4 us (16%)
  between operations  32.4 us (16%)
  local copies, waits for them, and re-layouts  27.4 us (13%)
  blocking collectives  25.5 us (12%)
  other arithmetic  5.07 us (2%)
    all_to_all x1, waiting for transfers between devices, shards(): lax.all_to_all(slot_grad.reshape(peers, slots, tile, width), 'col', split...  28.2 us
    all_gather x1, blocking collectives, shards(): gathered = lax.all_gather(picked, 'row', axis=0, tiled=False)  25.5 us
    dot_general x6, matrix products, shards(): lax.dot_general(adjacency[section], agg_grad, (((0,), (0,)), ((), ())), p...  14.8 us
    unnamed x69, local copies, waits for them, and re-layouts  13.7 us
    all_to_all x1, waiting for transfers between devices, shards(): lax.all_to_all(partials, 'row', split_axis=1, concat_axis=1, tiled=True)  8.89 us
    all_to_all x1, starting transfers between devices, shards(): lax.all_to_all(features[:hub_rows].reshape(rows_n, part, width), 'row', s...  8.59 us
    all_to_all x1, starting transfers between devices, shards(): lax.all_to_all(outgoing, 'col', split_axis=0, concat_axis=0, tiled=True)  8.33 us
    all_to_all x1, starting transfers between devices, shards(): lax.all_to_all(slot_grad.reshape(peers, slots, tile, width), 'col', split...  6.92 us
  transfers between devices with their start and end apart: 5, of which 3 were waited for; matrix products, arithmetic and copies ran while one was open for 17% of the time, Pallas kernels for 0%

commit v1 on v0

--- a/solution.py
+++ b/solution.py
@@ -91,7 +91,10 @@
             for section in range(sections)
         ]
     ).reshape(sections, rows_n, part, width)
-    landed = lax.all_to_all(partials, "row", split_axis=1, concat_axis=1, tiled=True)
+    landed = jnp.concatenate(
+        lax.all_to_all(jnp.stack(jnp.split(partials, lax.axis_size("row"), axis=1)), "row", 0, 0),
+        axis=1,
+    )
     summed = jnp.sum(landed.astype(f32), axis=1)
     owners = (hub_ids[None, :] == jnp.arange(rows_n, dtype=jnp.int32)[:, None]).astype(f32)
     to_owner = jnp.sum(owners[:, :, None, None] * summed[None], axis=1).astype(bf16)

time: 206 us -> 221 us (1.073)
  local copies, waits for them, and re-layouts: 27.4 us -> 43.6 us
  matrix products: 38.4 us -> 34.4 us
  waiting for transfers between devices: 42.1 us -> 45.4 us
    unnamed x69 -> x100, local copies, waits for them, and re-layouts: 13.7 us -> 29.3 us
    dot_general x6, matrix products: 14.8 us -> 10.9 us  [shards(): lax.dot_general(adjacency[section], agg_grad, (((0,), (0,)), ((), ())), p...]
    all_to_all x1, waiting for transfers between devices: 8.89 us -> 12.2 us  [shards(): lax.all_to_all(jnp.stack(jnp.split(partials, lax.axis_size('row'), axis=1...]
  transfers between devices with their start and end apart: 5 -> 5, of which waited for: 3 -> 3; matrix products, arithmetic and copies ran while one was open for 17% -> 14% of each run, Pallas kernels for 0% -> 0%
where the time goes in v1:
time: 221 us; the launch traced here: 220 us
  waiting for transfers between devices  45.4 us (21%)
  local copies, waits for them, and re-layouts  43.6 us (20%)
  matrix products  34.4 us (16%)
  starting transfers between devices  33.3 us (15%)
  between operations  32.5 us (15%)
  blocking collectives  25.5 us (12%)
  other arithmetic  5.07 us (2%)
    unnamed x100, local copies, waits for them, and re-layouts  29.3 us
    all_to_all x1, waiting for transfers between devices, shards(): lax.all_to_all(slot_grad.reshape(peers, slots, tile, width), 'col', split...  28.2 us
    all_gather x1, blocking collectives, shards(): gathered = lax.all_gather(picked, 'row', axis=0, tiled=False)  25.5 us
    all_to_all x1, waiting for transfers between devices, shards(): lax.all_to_all(jnp.stack(jnp.split(partials, lax.axis_size('row'), axis=1...  12.2 us
    dot_general x6, matrix products, shards(): lax.dot_general(adjacency[section], agg_grad, (((0,), (0,)), ((), ())), p...  10.9 us
    all_to_all x1, starting transfers between devices, shards(): lax.all_to_all(features[:hub_rows].reshape(rows_n, part, width), 'row', s...  8.59 us
    all_to_all x1, starting transfers between devices, shards(): lax.all_to_all(outgoing, 'col', split_axis=0, concat_axis=0, tiled=True)  8.33 us
    all_to_all x1, starting transfers between devices, shards(): lax.all_to_all(slot_grad.reshape(peers, slots, tile, width), 'col', split...  6.92 us
  transfers between devices with their start and end apart: 5, of which 3 were waited for; matrix products, arithmetic and copies ran while one was open for 14% of the time, Pallas kernels for 0%

profile of v1, /device:TPU:1, one launch (start us, length us, event | category | flops | bytes accessed | tf_op | source)
XLA Modules:
  0.0 219.8 jit_solution(4971217499120939832)
XLA Ops:
  0.7 1.7 slice_bitcast_fusion.13
  2.3 8.6 %all-to-all-start.1 = ((bf16[32,8,256]{2,1,0:T(8,128)(2,1)}), bf16[32,8,256]{2,1,0:T(8,128)(2,1)S(1)}, u32[]{:S(2)}, u32[]{:S(2)}) async-start(bf16[32,8,256]{2,1,0:T(8,128)(2,1)} %slice_bitcast_fusion.13), calls=%async_computation.1 | async-start | bytes 262144 | tf_op jit(solution)/shard_map/all_to_all | solution.py:31
  10.9 0.8 copy.244
  11.8 0.7 fusion.67
  22.6 1.6 fusion.66
  31.7 0.8 copy.243
  32.5 0.7 fusion.65
  43.1 0.9 constant_dynamic-update-slice_fusion.15
  44.0 0.8 constant_dynamic-update-slice_fusion.14
  44.9 0.8 constant_dynamic-update-slice_fusion.13
  45.7 0.8 constant_dynamic-update-slice_fusion.12
  46.6 0.8 constant_dynamic-update-slice_fusion.11
  47.4 0.8 constant_dynamic-update-slice_fusion.10
  48.3 0.8 constant_dynamic-update-slice_fusion.9
  49.1 0.8 constant_dynamic-update-slice_fusion.8
  49.9 0.8 constant_dynamic-update-slice_fusion.7
  50.9 1.3 copy.245
  52.7 3.7 %convert_reduce_fusion = f32[2048]{0:T(1024)S(1)} fusion(bf16[1,6,2048,256]{3,2,1,0:T(8,128)(2,1)} %param.16), kind=kLoop, calls=%fused_computation | loop fusion | flops 6289408 | bytes 6299648 | tf_op jit(solution)/shard_map/reduce_sum | solution.py:71
  56.4 1.8 fusion.70
  62.2 8.3 %all-to-all-start = ((bf16[8,2,128,256]{2,3,1,0:T(8,128)(2,1)}), bf16[8,2,128,256]{2,3,1,0:T(8,128)(2,1)}, u32[]{:S(2)}, u32[]{:S(2)}) async-start(bf16[8,2,128,256]{2,3,1,0:T(8,128)(2,1)} %copy.245), calls=%async_computation | async-start | bytes 2097152 | tf_op jit(solution)/shard_map/all_to_all | solution.py:50
  70.6 25.5 %all-gather = bf16[192,8,256]{2,1,0:T(8,128)(2,1)S(1)} all-gather(bf16[6,8,256]{2,1,0:T(8,128)(2,1)S(1)} %constant_dynamic-update-slice_fusion.16), channel_id=2, replica_groups=mesh['row'=32,'col'=8] {'row'}, dimensions={0}, use_global_device_ids=true | all-gather | bytes 811008 | tf_op jit(solution)/shard_map/all_gather | solution.py:41
  96.1 1.9 fusion.33
  98.0 1.7 convolution_add_fusion.6
  100.8 1.8 convolution_add_fusion.3
  102.6 3.0 %convolution_bitcast_fusion = f32[16,128,256]{1,2,0:T(8,128)} fusion(bf16[16,128,256]{1,2,0:T(8,128)(2,1)} %bitcast.35, bf16[16,128,128]{2,1,0:T(8,128)(2,1)S(1)} %bitcast.447), kind=kOutput, calls=%fused_computation.21 | convolution fusion | flops 134217728 | bytes 3670016 | tf_op jit(solution)/shard_map/sij,sjd->sid/dot_general | solution.py:61
  105.6 2.2 %copy.246 = f32[16,128,256]{2,0,1:T(8,128)S(1)} copy(f32[16,128,256]{1,2,0:T(8,128)} %convolution_bitcast_fusion) | data formatting | bytes 4194304 | tf_op jit(solution)/shard_map/sij,sjd->sid/dot_general | solution.py:61
  107.9 2.5 %fusion.51 = f32[16,128,256]{2,0,1:T(8,128)S(1)} fusion(f32[16,128,256]{2,0,1:T(8,128)S(1)} %copy.246, f32[16]{0:T(128)} %copy-done.10, s32[16]{0:T(128)S(1)} %eq.45), kind=kOutput, calls=%fused_computation.190 | convolution fusion | flops 100663808 | bytes 4194432 | tf_op jit(solution)/shard_map/sn,sid->nid/dot_general | solution.py:64
  110.4 1.2 copy.247
  111.6 1.9 copy.248
  113.5 6.0 %multiply_convert_fusion.1 = (bf16[2048,256]{1,0:T(8,128)(2,1)S(1)}, bf16[2048,256]{1,0:T(8,128)(2,1)}) fusion(bf16[2048,256]{1,0:T(8,128)(2,1)} %param.21, f32[256]{0:T(256)S(1)} %copy-done.13, f32[2048,256]{1,0:T(8,128)} %fusion.70, bf16[256,256]{1,0:T(8,128)(2,1)S(1)} %copy-done, f32[2048,256]{0,1:T(8,128)} %copy.248, ...), kind=kOutput, calls=%fused_computation.18 | convolution fusion | flops 546308096 | bytes 10757120 | tf_op jit(solution)/shard_map/dot_general | solution.py:75
  120.4 2.1 fusion.9
  122.6 1.7 fusion.11
  124.3 1.7 fusion.13
  126.1 1.7 fusion.15
  127.8 1.7 fusion.17
  129.6 1.7 fusion.19
  150.2 0.6 constant_dynamic-update-slice_fusion.38
  150.9 5.1 %all-to-all-start.3 = ((bf16[32,6,1,8,256]{4,3,1,2,0:T(8,128)(2,1)}), bf16[32,6,1,8,256]{4,3,1,2,0:T(8,128)(2,1)S(1)}, u32[]{:S(2)}, u32[]{:S(2)}) async-start(bf16[32,6,1,8,256]{4,3,1,2,0:T(8,128)(2,1)} %constant_dynamic-update-slice_fusion.38), calls=%async_computation.3 | async-start | bytes 1572864 | tf_op jit(solution)/shard_map/all_to_all | solution.py:95
  156.6 1.4 multiply_convert_fusion
  158.0 12.2 %all-to-all-done.3 = bf16[32,6,1,8,256]{4,3,1,2,0:T(8,128)(2,1)S(1)} async-done(((bf16[32,6,1,8,256]{4,3,1,2,0:T(8,128)(2,1)}), bf16[32,6,1,8,256]{4,3,1,2,0:T(8,128)(2,1)S(1)}, u32[]{:S(2)}, u32[]{:S(2)}) %all-to-all-start.3) | async-done | bytes 786464 | tf_op jit(solution)/shard_map/all_to_all | solution.py:95
  170.2 6.9 %all-to-all-start.2 = ((bf16[8,2,128,256]{2,3,1,0:T(8,128)(2,1)}), bf16[8,2,128,256]{2,3,1,0:T(8,128)(2,1)S(1)}, u32[]{:S(2)}, u32[]{:S(2)}) async-start(bf16[8,2,128,256]{2,3,1,0:T(8,128)(2,1)} %bitcast.98), calls=%async_computation.2 | async-start | bytes 2097152 | tf_op jit(solution)/shard_map/all_to_all | solution.py:113
  177.3 0.9 multiply_reduce_fusion
  178.2 28.2 %all-to-all-done.2 = bf16[8,2,128,256]{2,3,1,0:T(8,128)(2,1)S(1)} async-done(((bf16[8,2,128,256]{2,3,1,0:T(8,128)(2,1)}), bf16[8,2,128,256]{2,3,1,0:T(8,128)(2,1)S(1)}, u32[]{:S(2)}, u32[]{:S(2)}) %all-to-all-start.2) | async-done | bytes 1048608 | tf_op jit(solution)/shard_map/all_to_all | solution.py:113
  206.4 4.3 %all-to-all-start.4 = ((bf16[32,8,256]{2,1,0:T(8,128)(2,1)}), bf16[32,8,256]{2,1,0:T(8,128)(2,1)S(1)}, u32[]{:S(2)}, u32[]{:S(2)}) async-start(bf16[32,8,256]{2,1,0:T(8,128)(2,1)} %multiply_reduce_fusion), calls=%async_computation.4 | async-start | bytes 262144 | tf_op jit(solution)/shard_map/all_to_all | solution.py:102
  210.7 0.9 copy.332
  212.1 1.2 copy.283
  213.3 5.0 %all-to-all-done.4 = bf16[32,8,256]{2,1,0:T(8,128)(2,1)S(1)} async-done(((bf16[32,8,256]{2,1,0:T(8,128)(2,1)}), bf16[32,8,256]{2,1,0:T(8,128)(2,1)S(1)}, u32[]{:S(2)}, u32[]{:S(2)}) %all-to-all-start.4) | async-done | bytes 131104 | tf_op jit(solution)/shard_map/all_to_all | solution.py:102
  218.3 1.4 fusion.4
  (107 shorter events, 22.9 us)
Async XLA Ops:
  0.6 112.9 %copy-start = (bf16[256,256]{1,0:T(8,128)(2,1)S(1)}, bf16[256,256]{1,0:T(8,128)(2,1)}, u32[]{:S(2)}) copy-start(bf16[256,256]{1,0:T(8,128)(2,1)} %param.13) | copy-start | bytes 393220
  0.6 50.1 %copy-start.1 = (bf16[2048,256]{1,0:T(8,128)(2,1)S(1)}, bf16[2048,256]{1,0:T(8,128)(2,1)}, u32[]{:S(2)}) copy-start(bf16[2048,256]{1,0:T(8,128)(2,1)} %param.11) | copy-start | bytes 3145732
  2.3 59.8 %all-to-all-start.1 = ((bf16[32,8,256]{2,1,0:T(8,128)(2,1)}), bf16[32,8,256]{2,1,0:T(8,128)(2,1)S(1)}, u32[]{:S(2)}, u32[]{:S(2)}) async-start(bf16[32,8,256]{2,1,0:T(8,128)(2,1)} %slice_bitcast_fusion.13), calls=%async_computation.1 | async-start | bytes 262144 | tf_op jit(solution)/shard_map/all_to_all | solution.py:31
  43.1 9.2 %copy-start.12 = (s32[1,8]{1,0:T(1,128)S(1)}, s32[1,8]{1,0:T(1,128)}, u32[]{:S(2)}) copy-start(s32[1,8]{1,0:T(1,128)} %param.18) | copy-start | bytes 100
  43.1 9.3 %copy-start.2 = (bf16[1,8,2,128,128]{4,3,2,1,0:T(8,128)(2,1)S(1)}, bf16[1,8,2,128,128]{4,3,2,1,0:T(8,128)(2,1)}, u32[]{:S(2)}) copy-start(bf16[1,8,2,128,128]{4,3,2,1,0:T(8,128)(2,1)} %param.20) | copy-start | bytes 1572868
  52.4 9.6 %copy-start.10 = (f32[16]{0:T(128)}, f32[16]{0:T(128)S(1)}, u32[]{:S(2)}) copy-start(f32[16]{0:T(128)S(1)} %reshape.211) | copy-start | bytes 196
  52.6 3.7 %copy-start.7 = (bf16[256,256]{1,0:T(8,128)(2,1)S(1)}, bf16[256,256]{1,0:T(8,128)(2,1)}, u32[]{:S(2)}) copy-start(bf16[256,256]{1,0:T(8,128)(2,1)} %param.12) | copy-start | bytes 393220
  62.2 37.6 %slice-start = ((s8[6291456]{0:T(1024)(128)(4,1)}), s8[2097152]{0:T(1024)(128)(4,1)S(1)}, s32[]{:S(2)}) async-start(s8[6291456]{0:T(1024)(128)(4,1)} %bitcast.443), calls=%async_computation.5 | async-start | bytes 4194304
  62.2 40.4 %all-to-all-start = ((bf16[8,2,128,256]{2,3,1,0:T(8,128)(2,1)}), bf16[8,2,128,256]{2,3,1,0:T(8,128)(2,1)}, u32[]{:S(2)}, u32[]{:S(2)}) async-start(bf16[8,2,128,256]{2,3,1,0:T(8,128)(2,1)} %copy.245), calls=%async_computation | async-start | bytes 2097152 | tf_op jit(solution)/shard_map/all_to_all | solution.py:50
  96.1 3.6 %slice-start.1 = ((s8[6291456]{0:T(1024)(128)(4,1)}), s8[4194304]{0:T(1024)(128)(4,1)S(1)}, s32[]{:S(2)}) async-start(s8[6291456]{0:T(1024)(128)(4,1)} %bitcast.443), calls=%async_computation.6 | async-start | bytes 8388608
  111.6 1.9 copy-start.13
  119.5 1.0 copy-start.3
  120.4 9.2 %copy-start.5 = (bf16[2048,256]{0,1:T(8,128)(2,1)}, bf16[2048,256]{0,1:T(8,128)(2,1)S(1)}, u32[]{:S(2)}) copy-start(bf16[2048,256]{0,1:T(8,128)(2,1)S(1)} %fusion.5) | copy-start | bytes 3145732
  131.4 24.6 %copy-start.6 = (bf16[2048,256]{0,1:T(8,128)(2,1)S(1)}, bf16[2048,256]{0,1:T(8,128)(2,1)}, u32[]{:S(2)}) copy-start(bf16[2048,256]{0,1:T(8,128)(2,1)} %copy-done.5) | copy-start | bytes 3145732
  144.8 11.9 %copy-start.11 = (f32[16]{0:T(128)S(1)}, f32[16]{0:T(128)}, u32[]{:S(2)}) copy-start(f32[16]{0:T(128)} %copy-done.10) | copy-start | bytes 196
  150.9 19.3 %all-to-all-start.3 = ((bf16[32,6,1,8,256]{4,3,1,2,0:T(8,128)(2,1)}), bf16[32,6,1,8,256]{4,3,1,2,0:T(8,128)(2,1)S(1)}, u32[]{:S(2)}, u32[]{:S(2)}) async-start(bf16[32,6,1,8,256]{4,3,1,2,0:T(8,128)(2,1)} %constant_dynamic-update-slice_fusion.38), calls=%async_computation.3 | async-start | bytes 1572864 | tf_op jit(solution)/shard_map/all_to_all | solution.py:95
  156.6 20.5 %copy-start.9 = (s32[6]{0:T(128)S(1)}, s32[6]{0:T(128)}, u32[]{:S(2)}) copy-start(s32[6]{0:T(128)} %param.15) | copy-start | bytes 76
  170.2 36.2 %all-to-all-start.2 = ((bf16[8,2,128,256]{2,3,1,0:T(8,128)(2,1)}), bf16[8,2,128,256]{2,3,1,0:T(8,128)(2,1)S(1)}, u32[]{:S(2)}, u32[]{:S(2)}) async-start(bf16[8,2,128,256]{2,3,1,0:T(8,128)(2,1)} %bitcast.98), calls=%async_computation.2 | async-start | bytes 2097152 | tf_op jit(solution)/shard_map/all_to_all | solution.py:113
  206.4 12.0 %all-to-all-start.4 = ((bf16[32,8,256]{2,1,0:T(8,128)(2,1)}), bf16[32,8,256]{2,1,0:T(8,128)(2,1)S(1)}, u32[]{:S(2)}, u32[]{:S(2)}) async-start(bf16[32,8,256]{2,1,0:T(8,128)(2,1)} %multiply_reduce_fusion), calls=%async_computation.4 | async-start | bytes 262144 | tf_op jit(solution)/shard_map/all_to_all | solution.py:102
  212.0 6.3 %copy-start.4 = (bf16[2048,256]{1,0:T(8,128)(2,1)S(1)}, bf16[2048,256]{1,0:T(8,128)(2,1)}, u32[]{:S(2)}) copy-start(bf16[2048,256]{1,0:T(8,128)(2,1)} %copy-done.3) | copy-start | bytes 3145732
  212.0 6.3 %copy-start.8 = (bf16[256,256]{1,0:T(8,128)(2,1)S(1)}, bf16[256,256]{1,0:T(8,128)(2,1)}, u32[]{:S(2)}) copy-start(bf16[256,256]{1,0:T(8,128)(2,1)} %param.12) | copy-start | bytes 393220
